TPU v7x, 128 devices: a whole 4x4x4 slice. The times are simulated.
128 devices in a mesh: member: 8 (over y, x_lo), patch: 16 (over z, x_hi, core).
Axes of the slice: x: 4 (x_hi: 2, x_lo: 2; x = x_hi * 2 + x_lo), y: 4, z: 4, core: 2. Of those that a mesh axis runs over, the one named last changes fastest.
Arguments:
- fields: bfloat16 [128, 80, 64, 512], P(None, 'member', 'patch'), may hold values from -6 to 6
- block_device: int32 [128], replicated, may hold values from 0 to 127, each once
- weights: bfloat16 [128, 8, 80, 80], P(('member', 'patch')), may hold values from -0.3984375 to 1.59375
- control_increment: float32 [128, 64, 512], P(None, 'patch'), may hold values from -3 to 3
Outputs:
- analysis: bfloat16 [128, 80, 64, 512], P(None, 'member', 'patch')
All inputs are finite; a program needn't handle non-finite values.
Results may differ from a plain program's by a relative error of at most 0.0054.
Values may be sent and summed in bfloat16 or wider, within the bound.
A program may use at most 128 MiB of HBM per device.

v0:
```python
import jax
import jax.numpy as jnp
from jax import lax
from jax.sharding import PartitionSpec as P

RELAXATION = 0.85
EPSILON = 1e-06


def analyse(gathered, transform):
    members, rows, width = gathered.shape
    patches = transform.shape[0]
    values = gathered.astype(jnp.float32)
    prior_mean = jnp.mean(values, axis=0)
    perturb = values - prior_mean
    prior_spread = jnp.mean(perturb * perturb, axis=0)
    rounded = perturb.astype(jnp.bfloat16).reshape(members, patches, rows // patches, width)
    transformed = jnp.einsum(
        "kqrc,qkj->jqrc", rounded, transform, preferred_element_type=jnp.float32
    )
    transformed = transformed.reshape(members, rows, width)
    centered = transformed - jnp.mean(transformed, axis=0)
    posterior_spread = jnp.mean(centered * centered, axis=0)
    factor = RELAXATION * jnp.sqrt((prior_spread + EPSILON) / (posterior_spread + EPSILON)) + (
        1.0 - RELAXATION
    )
    return (prior_mean + factor * centered).astype(jnp.bfloat16)


def per_device(fields, block_device, weights, control_increment):
    block_count, local_members, band_rows, block_width = fields.shape
    groups = lax.axis_size("member")
    band_count = lax.axis_size("patch")
    owners = (
        jnp.zeros((block_count,), jnp.int32)
        .at[block_device]
        .set(jnp.arange(block_count, dtype=jnp.int32))
    )
    ordered = jnp.take(fields, owners, axis=0)
    gathered = lax.all_to_all(
        lax.all_to_all(ordered, "member", split_axis=0, concat_axis=1, tiled=True),
        "patch",
        split_axis=0,
        concat_axis=2,
        tiled=True,
    )
    result = analyse(gathered[0], weights[0])
    returned = lax.all_to_all(
        lax.all_to_all(result[None], "member", split_axis=1, concat_axis=0, tiled=True),
        "patch",
        split_axis=2,
        concat_axis=0,
        tiled=True,
    )
    positions = block_device % band_count * groups + block_device // band_count
    restored = jnp.take(returned, positions, axis=0)
    return (restored.astype(jnp.float32) + control_increment[:, None]).astype(jnp.bfloat16)


def solution(mesh):
    return jax.shard_map(
        per_device,
        mesh=mesh,
        in_specs=(
            P(None, "member", "patch", None),
            P(),
            P(("member", "patch"), None, None, None),
            P(None, "patch", None),
        ),
        out_specs=P(None, "member", "patch", None),
        check_vma=False,
    )
```

profile of v0, /device:TPU:1, one launch (start us, length us, event | category | flops | bytes accessed | tf_op | source)
XLA Modules:
  0.0 367.1 jit_solution(3912439791870108486)
XLA Ops:
  0.0 0.0 copy-start
  0.0 0.7 compare_select_fusion.5
  0.7 1.0 scatter_custom_fusion
  1.7 11.2 %gather_fusion = bf16[128,10,4,512]{3,2,1,0:T(4,128)(2,1)} fusion(bf16[128,10,4,512]{3,2,1,0:T(4,128)(2,1)} %param.6, s32[1024]{0:T(1024)S(1)} %pad_clamp_fusion.1), kind=kCustom, calls=%fused_computation.clone | custom fusion | bytes 10486272 | tf_op jit(solution)/shard_map/jit(_take)/gather | solution.py:39
  12.9 4.9 %broadcast_select_fusion = bf16[128,10,4,512]{3,2,1,0:T(4,128)(2,1)S(1)} fusion(bf16[128,10,4,512]{3,2,1,0:T(4,128)(2,1)} %gather_fusion, pred[128]{0:T(512)(128)(4,1)S(1)} %compare_and_fusion.1), kind=kLoop, calls=%fused_computation.21 | loop fusion | flops 2621440 | bytes 10485888 | tf_op jit(solution)/shard_map/jit(_take)/select_n | solution.py:39
  17.9 66.8 %all_to_all.57 = bf16[128,10,4,512]{3,2,1,0:T(4,128)(2,1)S(1)} all-to-all(bf16[128,10,4,512]{3,2,1,0:T(4,128)(2,1)S(1)} %broadcast_select_fusion), channel_id=1, replica_groups=mesh['member'=8,'patch'=16] {'member'}, dimensions={0} | all-to-all | bytes 10485760 | tf_op jit(solution)/shard_map/all_to_all | solution.py:41
  84.7 1.8 copy.55
  86.5 0.8 copy.56
  87.4 4.0 %copy.57 = bf16[16,80,4,512]{3,2,1,0:T(4,128)(2,1)S(1)} copy(bf16[16,80,4,512]{3,0,2,1:T(8,128)(2,1)S(1)} %bitcast.57) | data formatting | bytes 10485760 | tf_op jit(solution)/shard_map/all_to_all | solution.py:41
  91.4 71.0 %all_to_all.58 = bf16[16,80,4,512]{3,2,1,0:T(4,128)(2,1)S(1)} all-to-all(bf16[16,80,4,512]{3,2,1,0:T(4,128)(2,1)S(1)} %copy.57), channel_id=1, replica_groups=mesh['member'=8,'patch'=16] {'patch'}, dimensions={0} | all-to-all | bytes 10485760 | tf_op jit(solution)/shard_map/all_to_all | solution.py:40
  162.4 0.0 copy-start.2
  162.4 2.4 copy-done.2
  164.8 1.6 bitcast_reduce_fusion.1
  166.4 0.1 copy_multiply_fusion.1
  166.5 0.1 copy.60
  166.7 5.1 %fusion.3 = f32[16,4,512]{2,1,0:T(4,128)S(1)} fusion(f32[16,4,512]{2,1,0:T(4,128)S(1)} %copy.60, bf16[16,80,4,512]{3,2,1,0:T(4,128)(2,1)} %copy-done.2), kind=kLoop, calls=%fused_computation.10 | loop fusion | flops 10452992 | bytes 5505024 | tf_op jit(solution)/shard_map/reduce_sum | solution.py:16
  171.7 0.1 fusion.10
  171.8 0.1 copy.63
  172.0 8.1 %bitcast_convert_fusion = f32[16,1,80,4,512]{4,2,3,0,1:T(8,128)} fusion(bf16[16,80,4,512]{3,2,1,0:T(4,128)(2,1)} %copy-done.2), kind=kLoop, calls=%fused_computation.19 | loop fusion | flops 2621440 | bytes 15728640 | tf_op jit(solution)/shard_map/convert_element_type | solution.py:13
  180.1 0.0 copy-done
  180.1 6.0 %bitcast_reduce_fusion = (f32[8,8,512]{2,1,0:T(8,128)S(1)}, f32[8,8,512,80]{2,3,1,0:T(8,128)S(1)}) fusion(bf16[1,8,80,80]{3,2,1,0:T(8,128)(2,1)S(1)} %copy-done, f32[80,8,8,512]{3,0,2,1:T(8,128)} %bitcast.55, f32[8,8,512]{2,1,0:T(8,128)S(1)} %div.40), kind=kOutput, calls=%fused_computation.4 | convolution fusion | flops 427261952 | bytes 21336064 | tf_op jit(solution)/shard_map/kqrc,qkj->jqrc/dot_general | solution.py:18
  186.1 2.6 fusion.1
  188.7 0.1 fusion.13
  188.8 8.7 %fusion.6 = bf16[1,80,64,512]{3,2,0,1:T(8,128)(2,1)} fusion(f32[1,80,64,512]{3,1,2,0:T(8,128)S(1)} %bitcast.54, f32[64,512]{1,0:T(8,128)S(1)} %get-tuple-element.9, f32[64,512]{1,0:T(8,128)S(1)} %fusion.13, f32[64,512]{1,0:T(8,128)S(1)} %div.38), kind=kLoop, calls=%fused_computation.14 | loop fusion | flops 10485760 | bytes 16121856 | tf_op jit(solution)/shard_map/convert_element_type | solution.py:27
  197.5 63.2 %all_to_all.59 = bf16[1,80,64,512]{3,2,0,1:T(8,128)(2,1)S(1)} all-to-all(bf16[1,80,64,512]{3,2,0,1:T(8,128)(2,1)} %fusion.6), channel_id=1, replica_groups=mesh['member'=8,'patch'=16] {'member'}, dimensions={1} | all-to-all | bytes 10485760 | tf_op jit(solution)/shard_map/all_to_all | solution.py:49
  260.7 5.3 %copy.67 = bf16[8,10,64,512]{3,0,1,2:T(8,128)(2,1)} copy(bf16[8,10,64,512]{3,2,1,0:T(8,128)(2,1)S(1)} %bitcast.58) | data formatting | bytes 10485760 | tf_op jit(solution)/shard_map/all_to_all | solution.py:49
  266.0 0.0 copy-start.4
  266.0 6.9 %all-to-all-start.3 = ((bf16[8,10,64,512]{3,0,1,2:T(8,128)(2,1)}), bf16[8,10,64,512]{3,0,1,2:T(8,128)(2,1)}, u32[]{:S(2)}, u32[]{:S(2)}) async-start(bf16[8,10,64,512]{3,0,1,2:T(8,128)(2,1)} %copy.67), calls=%async_computation.3 | async-start | bytes 10485760 | tf_op jit(solution)/shard_map/all_to_all | solution.py:48
  272.9 0.0 copy-done.4
  272.9 62.2 %all-to-all-done.3 = bf16[8,10,64,512]{3,0,1,2:T(8,128)(2,1)} async-done(((bf16[8,10,64,512]{3,0,1,2:T(8,128)(2,1)}), bf16[8,10,64,512]{3,0,1,2:T(8,128)(2,1)}, u32[]{:S(2)}, u32[]{:S(2)}) %all-to-all-start.3) | async-done | bytes 5242912 | tf_op jit(solution)/shard_map/all_to_all | solution.py:48
  335.1 3.2 copy.92
  338.4 6.4 %copy.70 = bf16[128,10,4,512]{3,2,1,0:T(4,128)(2,1)} copy(bf16[128,10,4,512]{3,0,2,1:T(8,128)(2,1)S(1)} %bitcast.59) | data formatting | bytes 10485760 | tf_op jit(solution)/shard_map/all_to_all | solution.py:48
  344.8 0.0 copy-start.3
  344.8 11.6 %gather_fusion.1 = bf16[128,10,4,512]{3,2,1,0:T(4,128)(2,1)} fusion(bf16[128,10,4,512]{3,2,1,0:T(4,128)(2,1)} %copy.70, s32[1024]{0:T(1024)S(1)} %pad_clamp_fusion), kind=kCustom, calls=%fused_computation.1.clone | custom fusion | bytes 10486272 | tf_op jit(solution)/shard_map/jit(_take)/gather | solution.py:56
  356.4 0.0 copy-start.1
  356.4 0.0 copy-done.3
  356.4 10.3 %add_convert_fusion = bf16[128,10,4,512]{3,2,1,0:T(4,128)(2,1)} fusion(bf16[128,10,4,512]{3,2,1,0:T(4,128)(2,1)} %gather_fusion.1, f32[128,4,512]{2,1,0:T(4,128)S(1)} %copy-done.3, pred[128]{0:T(512)(128)(4,1)S(1)} %get-tuple-element.6), kind=kLoop, calls=%fused_computation.15 | loop fusion | flops 10485760 | bytes 11534464 | tf_op jit(solution)/shard_map/convert_element_type | solution.py:57
  366.6 0.0 copy-done.1
  (10 shorter events, 0.2 us)
Async XLA Ops:
  0.0 180.1 %copy-start = (bf16[1,8,80,80]{3,2,1,0:T(8,128)(2,1)S(1)}, bf16[1,8,80,80]{3,2,1,0:T(8,128)(2,1)}, u32[]{:S(2)}) copy-start(bf16[1,8,80,80]{3,2,1,0:T(8,128)(2,1)} %param.8) | copy-start | bytes 307204
  162.4 2.4 copy-start.2
  266.0 6.9 %copy-start.4 = (s32[128]{0:T(128)S(1)}, s32[128]{0:T(128)}, u32[]{:S(2)}) copy-start(s32[128]{0:T(128)} %param.7) | copy-start | bytes 1540
  266.0 69.2 %all-to-all-start.3 = ((bf16[8,10,64,512]{3,0,1,2:T(8,128)(2,1)}), bf16[8,10,64,512]{3,0,1,2:T(8,128)(2,1)}, u32[]{:S(2)}, u32[]{:S(2)}) async-start(bf16[8,10,64,512]{3,0,1,2:T(8,128)(2,1)} %copy.67), calls=%async_computation.3 | async-start | bytes 10485760 | tf_op jit(solution)/shard_map/all_to_all | solution.py:48
  344.8 11.6 %copy-start.3 = (f32[128,4,512]{2,1,0:T(4,128)S(1)}, f32[128,4,512]{2,1,0:T(4,128)}, u32[]{:S(2)}) copy-start(f32[128,4,512]{2,1,0:T(4,128)} %param.9) | copy-start | bytes 3145732
  356.4 10.3 %copy-start.1 = (bf16[1,8,80,80]{3,2,1,0:T(8,128)(2,1)S(1)}, bf16[1,8,80,80]{3,2,1,0:T(8,128)(2,1)}, u32[]{:S(2)}) copy-start(bf16[1,8,80,80]{3,2,1,0:T(8,128)(2,1)} %param.8) | copy-start | bytes 307204
where the time goes:
time: 373 us; the launch traced here: 367 us
  blocking collectives  201 us (54%)
  waiting for transfers between devices  62.2 us (17%)
  local copies, waits for them, and re-layouts  48.1 us (13%)
  other arithmetic  42.3 us (11%)
  starting transfers between devices  6.92 us (2%)
  matrix products  5.98 us (2%)
    all_to_all x1, blocking collectives, per_device(): lax.all_to_all(lax.all_to_all(ordered, 'member', split_axis=0, concat_axi...  71 us
    all_to_all x1, blocking collectives, per_device(): lax.all_to_all(ordered, 'member', split_axis=0, concat_axis=1, tiled=True)  66.8 us
    all_to_all x1, blocking collectives, per_device(): lax.all_to_all(result[None], 'member', split_axis=1, concat_axis=0, tiled...  63.2 us
    all_to_all x1, waiting for transfers between devices, per_device(): lax.all_to_all(lax.all_to_all(result[None], 'member', split_axis=1, conca...  62.2 us
    gather x1, local copies, waits for them, and re-layouts, per_device(): restored = jnp.take(returned, positions, axis=0)  11.6 us
    gather x1, local copies, waits for them, and re-layouts, per_device(): ordered = jnp.take(fields, owners, axis=0)  11.2 us
    convert_element_type x1, other arithmetic, per_device(): (restored.astype(jnp.float32) + control_increment[:, None]).astype(jnp.bf...  10.3 us
    all_to_all x2, local copies, waits for them, and re-layouts, per_device(): lax.all_to_all(lax.all_to_all(result[None], 'member', split_axis=1, conca...  9.61 us
  transfers between devices with their start and end apart: 1, of which 1 were waited for; matrix products, arithmetic and copies ran while one was open for 0% of the time, Pallas kernels for 0%

commit v1 on v0

v1 whole, which is shorter than its diff:
```python
import functools

import jax
import jax.numpy as jnp
from jax import lax
from jax.experimental import pallas as pl
from jax.experimental.pallas import tpu as pltpu
from jax.sharding import PartitionSpec as P

RELAXATION = 0.85
EPSILON = 1e-06
MESH = pl.DeviceIdType.MESH
LANES = 128


def wait_bytes(ref, sem):
    pltpu.make_async_copy(ref, ref, sem).wait()


def analyse(gathered, transform, control, pert, moved, result, members, rows):
    zero = jnp.zeros((rows, LANES), jnp.float32)

    def add(k, total):
        return total + gathered[k].astype(jnp.float32)

    prior_mean = lax.fori_loop(0, members, add, zero, unroll=8) / members

    def perturb(k, total):
        value = gathered[k].astype(jnp.float32) - prior_mean
        pert[pl.ds(pl.multiple_of(k * rows, rows), rows), :] = value
        return total + value * value

    prior_spread = lax.fori_loop(0, members, perturb, zero, unroll=8) / members

    out_in = transform.astype(jnp.float32).T.astype(jnp.bfloat16)
    for s in range(0, rows, 2):
        both = jnp.concatenate(
            [pert[pl.ds(s + i, members, stride=rows), :].astype(jnp.bfloat16) for i in range(2)],
            axis=1,
        )
        product = jnp.dot(out_in, both, preferred_element_type=jnp.float32)
        for i in range(2):
            moved[pl.ds(s + i, members, stride=rows), :] = product[:, i * LANES : (i + 1) * LANES]

    def at(j):
        return moved[pl.ds(pl.multiple_of(j * rows, rows), rows), :]

    post_mean = lax.fori_loop(0, members, lambda j, t: t + at(j), zero, unroll=8) / members

    def square(j, total):
        centered = at(j) - post_mean
        return total + centered * centered

    posterior_spread = lax.fori_loop(0, members, square, zero, unroll=8) / members
    factor = RELAXATION * jnp.sqrt((prior_spread + EPSILON) / (posterior_spread + EPSILON)) + (
        1.0 - RELAXATION
    )

    def write(j, carry):
        member = (prior_mean + factor * (at(j) - post_mean)).astype(jnp.bfloat16)
        result[j] = (member.astype(jnp.float32) + control).astype(jnp.bfloat16)
        return carry

    lax.fori_loop(0, members, write, 0, unroll=8)


def exchange(
    groups, bands, patches,
    owners, fields, weights, control,
    returned,
    held, ordered, gathered, result, chosen, increments, pert, moved,
    load_sem, weight_sems, gather_send, gather_recv, return_sems,
):
    blocks, local, rows, _ = held.shape
    mine = blocks // groups
    members = groups * local
    group = lax.axis_index("member")
    band = lax.axis_index("patch")
    load_fields = pltpu.make_async_copy(fields, held, load_sem.at[0])
    load_control = pltpu.make_async_copy(control, increments, load_sem.at[1])
    load_fields.start()
    load_control.start()

    def other_group(i):
        return lax.rem(group + i, groups)

    def other_band(i):
        return lax.rem(band + i, bands)

    barrier = pltpu.get_barrier_semaphore()

    def greet_group(i, carry):
        pl.semaphore_signal(barrier, inc=1, device_id=(other_group(i), band), device_id_type=MESH)
        return carry

    def greet_band(i, carry):
        pl.semaphore_signal(barrier, inc=1, device_id=(group, other_band(i)), device_id_type=MESH)
        return carry

    lax.fori_loop(1, groups, greet_group, 0)
    lax.fori_loop(1, bands, greet_band, 0)
    pl.semaphore_wait(barrier, groups + bands - 2)

    per_patch = bands // patches

    def send_weights(i, carry):
        to = other_band(i)
        pltpu.make_async_remote_copy(
            src_ref=weights.at[to // per_patch],
            dst_ref=chosen.at[band],
            send_sem=weight_sems.at[0],
            recv_sem=weight_sems.at[1],
            device_id=(group, to),
            device_id_type=MESH,
        ).start()
        return carry

    lax.fori_loop(1, bands, send_weights, 0)
    own_weights = pltpu.make_async_copy(
        weights.at[band // per_patch], chosen.at[band], weight_sems.at[2]
    )
    own_weights.start()

    load_fields.wait()

    def send_block(c, carry):
        here = owners[group * mine + c]
        for k in range(local):
            gathered[c, group * local + k] = held[here, k]

        def to_peer(i, inner):
            to = other_group(i)
            block = owners[to * mine + c]
            for k in range(local):
                ordered[i - 1, c, k] = held[block, k]
            pltpu.make_async_remote_copy(
                src_ref=ordered.at[i - 1, c],
                dst_ref=gathered.at[c, pl.ds(group * local, local)],
                send_sem=gather_send,
                recv_sem=gather_recv.at[c],
                device_id=(to, band),
                device_id_type=MESH,
            ).start()
            return inner

        lax.fori_loop(1, groups, to_peer, 0)
        return carry

    lax.fori_loop(0, mine, send_block, 0)

    load_control.wait()
    own_weights.wait()
    wait_bytes(chosen.at[pl.ds(0, bands - 1)], weight_sems.at[1])

    def analyse_block(c, carry):
        wait_bytes(gathered.at[c, pl.ds(0, members - local)], gather_recv.at[c])
        slot = group * mine + c
        analyse(
            gathered.at[c], chosen[c], increments[owners[slot]],
            pert, moved, result.at[c], members, rows,
        )

        def to_peer(i, inner):
            to = other_group(i)
            pltpu.make_async_remote_copy(
                src_ref=result.at[c, pl.ds(to * local, local)],
                dst_ref=returned.at[slot],
                send_sem=return_sems.at[0],
                recv_sem=return_sems.at[1],
                device_id=(to, band),
                device_id_type=MESH,
            ).start()
            return inner

        lax.fori_loop(1, groups, to_peer, 0)
        pltpu.make_async_copy(
            result.at[c, pl.ds(group * local, local)], returned.at[slot], return_sems.at[2]
        ).start()
        return carry

    lax.fori_loop(0, mine, analyse_block, 0)

    sent = returned.at[pl.ds(0, blocks - mine)]
    wait_bytes(sent, return_sems.at[1])
    wait_bytes(returned.at[pl.ds(0, mine)], return_sems.at[2])
    wait_bytes(chosen.at[pl.ds(0, bands - 1)], weight_sems.at[0])
    wait_bytes(ordered, gather_send)
    wait_bytes(sent, return_sems.at[0])


def place(block_device, returned, analysis, sem):
    blocks = returned.shape[0]

    def one(b, carry):
        pltpu.make_async_copy(returned.at[block_device[b]], analysis.at[b], sem).start()
        return carry

    lax.fori_loop(0, blocks, one, 0)
    wait_bytes(returned, sem)


def per_device(groups, bands, fields, block_device, weights, control_increment):
    blocks, local, band_rows, width = fields.shape
    patches, members = weights.shape[1], weights.shape[2]
    pieces = width // LANES
    rows = pieces * band_rows
    tiled = (
        fields.reshape(blocks, local, band_rows, pieces, LANES)
        .transpose(0, 1, 3, 2, 4)
        .reshape(blocks, local, rows, LANES)
    )
    control = (
        control_increment.reshape(blocks, band_rows, pieces, LANES)
        .transpose(0, 2, 1, 3)
        .reshape(blocks, rows, LANES)
    )
    index = jnp.arange(blocks, dtype=jnp.int32)
    owners = jnp.sum(
        jnp.where(block_device[None, :] == index[:, None], index[None, :], 0), axis=1
    ).astype(jnp.int32)
    mine = blocks // groups
    any_space = pl.BlockSpec(memory_space=pl.ANY)
    smem = pl.BlockSpec(memory_space=pltpu.SMEM)
    half = jnp.bfloat16
    returned = pl.pallas_call(
        functools.partial(exchange, groups, bands, patches),
        out_shape=jax.ShapeDtypeStruct((blocks, local, rows, LANES), half),
        in_specs=[smem, any_space, any_space, any_space],
        out_specs=any_space,
        scratch_shapes=[
            pltpu.VMEM((blocks, local, rows, LANES), half),
            pltpu.VMEM((groups - 1, mine, local, rows, LANES), half),
            pltpu.VMEM((mine, members, rows, LANES), half),
            pltpu.VMEM((mine, members, rows, LANES), half),
            pltpu.VMEM((bands, members, members), half),
            pltpu.VMEM((blocks, rows, LANES), jnp.float32),
            pltpu.VMEM((members * rows, LANES), jnp.float32),
            pltpu.VMEM((members * rows, LANES), jnp.float32),
            pltpu.SemaphoreType.DMA((2,)),
            pltpu.SemaphoreType.DMA((3,)),
            pltpu.SemaphoreType.DMA,
            pltpu.SemaphoreType.DMA((mine,)),
            pltpu.SemaphoreType.DMA((3,)),
        ],
        compiler_params=pltpu.CompilerParams(
            collective_id=0, has_side_effects=True, vmem_limit_bytes=48 * 2**20
        ),
        name="exchange",
    )(owners, tiled, weights[0], control)
    analysis = pl.pallas_call(
        place,
        out_shape=jax.ShapeDtypeStruct((blocks, local, rows, LANES), half),
        in_specs=[smem, any_space],
        out_specs=any_space,
        scratch_shapes=[pltpu.SemaphoreType.DMA],
        name="place",
    )(block_device, returned)
    return (
        analysis.reshape(blocks, local, pieces, band_rows, LANES)
        .transpose(0, 1, 3, 2, 4)
        .reshape(blocks, local, band_rows, width)
    )


def solution(mesh):
    return jax.shard_map(
        functools.partial(per_device, mesh.shape["member"], mesh.shape["patch"]),
        mesh=mesh,
        in_specs=(
            P(None, "member", "patch", None),
            P(),
            P(("member", "patch"), None, None, None),
            P(None, "patch", None),
        ),
        out_specs=P(None, "member", "patch", None),
        check_vma=False,
    )
```

time: 373 us -> 291 us (0.78); the launches traced: 367 us -> 290 us
  Pallas kernels: 0 us -> 287 us
  blocking collectives: 201 us -> 0 us
  waiting for transfers between devices: 62.2 us -> 0 us
  local copies, waits for them, and re-layouts: 48.1 us -> 2.14 us
  other arithmetic: 42.3 us -> 0.76 us
  starting transfers between devices: 6.92 us -> 0 us
  matrix products: 5.98 us -> 0 us
    pallas_call x0 -> x2, Pallas kernels: none -> 287 us  [the longest x1 161 us: per_device(): pl.pallas_call(place, out_shape=jax.ShapeDtypeStruct((blocks, local, rows...]
    all_to_all x3 -> x0, blocking collectives: 201 us -> none  [the longest x1 71 us: per_device(): lax.all_to_all(lax.all_to_all(ordered, 'member', split_axis=0, concat_axi...]
    all_to_all x1 -> x0, waiting for transfers between devices: 62.2 us -> none  [per_device(): lax.all_to_all(lax.all_to_all(result[None], 'member', split_axis=1, conca...]
    convert_element_type x3 -> x0, other arithmetic: 27.1 us -> none  [the longest x1 10.3 us: per_device(): (restored.astype(jnp.float32) + control_increment[:, None]).astype(jnp.bf...]
    gather x2 -> x0, local copies, waits for them, and re-layouts: 22.8 us -> none  [the longest x1 11.6 us: per_device(): restored = jnp.take(returned, positions, axis=0)]
    all_to_all x6 -> x0, local copies, waits for them, and re-layouts: 21.6 us -> none  [the longest x2 9.61 us: per_device(): lax.all_to_all(lax.all_to_all(result[None], 'member', split_axis=1, conca...]
    reduce_sum x3 -> x1, other arithmetic: 9.25 us -> 0.76 us  [per_device(): jnp.sum(jnp.where(block_device[None, :] == index[:, None], index[None, :]...]
    all_to_all x1 -> x0, starting transfers between devices: 6.92 us -> none  [per_device(): lax.all_to_all(lax.all_to_all(result[None], 'member', split_axis=1, conca...]
  transfers between devices with their start and end apart: 1 -> 0, of which waited for: 1 -> 0; matrix products, arithmetic and copies ran while one was open for 0% -> 0% of each run, Pallas kernels for 0% -> 0%
where the time goes in v1:
time: 291 us; the launch traced here: 290 us
  Pallas kernels  287 us (99%)
    pallas_call x1, Pallas kernels, per_device(): pl.pallas_call(place, out_shape=jax.ShapeDtypeStruct((blocks, local, rows...  161 us
    pallas_call x1, Pallas kernels, per_device(): pl.pallas_call(functools.partial(exchange, groups, bands, patches), out_s...  126 us

profile of v1, /device:TPU:1, one launch (start us, length us, event | category | flops | bytes accessed | tf_op | source)
XLA Modules:
  0.0 289.8 jit_solution(13252333698674608572)
XLA Ops:
  0.0 0.8 select_reduce_fusion.owners
  0.8 0.0 copy-start
  0.8 1.2 copy-done
  2.0 0.0 copy-start.1
  2.0 0.9 copy-done.1
  2.9 126.3 %exchange.1.returned = bf16[128,10,16,128]{3,2,1,0:T(8,128)(2,1)} custom-call(s32[128]{0:T(128)S(1)} %select_reduce_fusion.owners, bf16[128,10,16,128]{3,2,1,0:T(8,128)(2,1)} %bitcast.18, bf16[8,80,80]{2,1,0:T(8,128)(2,1)S(1)} %bitcast.17, f32[128,16,128]{2,1,0:T(8,128)S(1)} %bitcast.16), custom_call_target="tpu_custom_call" | custom-call | tf_op jit(solution)/shard_map/exchange/pallas_call | solution.py:225
  129.2 160.6 %place.1 = bf16[128,10,16,128]{3,2,1,0:T(8,128)(2,1)} custom-call(s32[128]{0:T(128)} %block_device.1, bf16[128,10,16,128]{3,2,1,0:T(8,128)(2,1)} %exchange.1.returned), custom_call_target="tpu_custom_call" | custom-call | tf_op jit(solution)/shard_map/place/pallas_call | solution.py:250
Async XLA Ops:
  0.8 1.2 copy-start
  2.0 0.9 copy-start.1

commit v2 on v1

--- a/solution.py
+++ b/solution.py
@@ -66,26 +66,38 @@
 
 def exchange(
     groups, bands, patches,
-    owners, fields, weights, control,
+    block_device, fields, weights, control,
     returned,
-    held, ordered, gathered, result, chosen, increments, pert, moved,
-    load_sem, weight_sems, gather_send, gather_recv, return_sems,
+    held, ordered, gathered, result, chosen, increments, pert, moved, owner_row, owners,
+    load_sems, weight_sems, gather_send, gather_recv, return_sems,
 ):
     blocks, local, rows, _ = held.shape
     mine = blocks // groups
     members = groups * local
     group = lax.axis_index("member")
     band = lax.axis_index("patch")
-    load_fields = pltpu.make_async_copy(fields, held, load_sem.at[0])
-    load_control = pltpu.make_async_copy(control, increments, load_sem.at[1])
-    load_fields.start()
-    load_control.start()
+    parts = 4
+
+    def load_fields(i):
+        part = pl.ds(i * (blocks // parts), blocks // parts)
+        return pltpu.make_async_copy(fields.at[part], held.at[part], load_sems.at[2 + i])
+
+    load_control = pltpu.make_async_copy(control, increments, load_sems.at[0])
+    for i in range(parts):
+        load_fields(i).start()
 
     def other_group(i):
         return lax.rem(group + i, groups)
 
-    def other_band(i):
-        return lax.rem(band + i, bands)
+    def half(of_band):
+        return lax.rem(of_band // 2, 2)
+
+    def weights_peer(i):
+        to = lax.rem(band + i, bands)
+        return group // 2 * 2 + lax.rem(group + half(band) + half(to), 2), to
+
+    def slot_of(to, i):
+        return (to // 2 * 2 + lax.rem(to + half(band) + half(i), 2)) * bands + i
 
     barrier = pltpu.get_barrier_semaphore()
 
@@ -94,23 +106,31 @@
         return carry
 
     def greet_band(i, carry):
-        pl.semaphore_signal(barrier, inc=1, device_id=(group, other_band(i)), device_id_type=MESH)
+        pl.semaphore_signal(barrier, inc=1, device_id=weights_peer(i), device_id_type=MESH)
         return carry
 
     lax.fori_loop(1, groups, greet_group, 0)
     lax.fori_loop(1, bands, greet_band, 0)
+
+    shape = (blocks, blocks)
+    match = block_device[...] == lax.broadcasted_iota(jnp.int32, shape, 0)
+    index = jnp.where(match, lax.broadcasted_iota(jnp.int32, shape, 1), 0)
+    owner_row[...] = jnp.max(index.T, axis=0, keepdims=True)
+    load_owners = pltpu.make_async_copy(owner_row, owners, load_sems.at[1])
+    load_owners.start()
+
     pl.semaphore_wait(barrier, groups + bands - 2)
 
     per_patch = bands // patches
 
     def send_weights(i, carry):
-        to = other_band(i)
+        to = weights_peer(i)
         pltpu.make_async_remote_copy(
-            src_ref=weights.at[to // per_patch],
+            src_ref=weights.at[to[1] // per_patch],
             dst_ref=chosen.at[band],
             send_sem=weight_sems.at[0],
             recv_sem=weight_sems.at[1],
-            device_id=(group, to),
+            device_id=to,
             device_id_type=MESH,
         ).start()
         return carry
@@ -121,16 +141,19 @@
     )
     own_weights.start()
 
-    load_fields.wait()
+    load_owners.wait()
+    for i in range(parts):
+        load_fields(i).wait()
+    load_control.start()
 
     def send_block(c, carry):
-        here = owners[group * mine + c]
+        here = owners[0, slot_of(group, c)]
         for k in range(local):
             gathered[c, group * local + k] = held[here, k]
 
         def to_peer(i, inner):
             to = other_group(i)
-            block = owners[to * mine + c]
+            block = owners[0, slot_of(to, c)]
             for k in range(local):
                 ordered[i - 1, c, k] = held[block, k]
             pltpu.make_async_remote_copy(
@@ -154,9 +177,9 @@
 
     def analyse_block(c, carry):
         wait_bytes(gathered.at[c, pl.ds(0, members - local)], gather_recv.at[c])
-        slot = group * mine + c
+        slot = slot_of(group, c)
         analyse(
-            gathered.at[c], chosen[c], increments[owners[slot]],
+            gathered.at[c], chosen[c], increments[owners[0, slot]],
             pert, moved, result.at[c], members, rows,
         )
 
@@ -173,29 +196,22 @@
             return inner
 
         lax.fori_loop(1, groups, to_peer, 0)
-        pltpu.make_async_copy(
-            result.at[c, pl.ds(group * local, local)], returned.at[slot], return_sems.at[2]
-        ).start()
+        for k in range(local):
+            returned[slot, k] = result[c, group * local + k]
         return carry
 
     lax.fori_loop(0, mine, analyse_block, 0)
 
     sent = returned.at[pl.ds(0, blocks - mine)]
     wait_bytes(sent, return_sems.at[1])
-    wait_bytes(returned.at[pl.ds(0, mine)], return_sems.at[2])
     wait_bytes(chosen.at[pl.ds(0, bands - 1)], weight_sems.at[0])
     wait_bytes(ordered, gather_send)
     wait_bytes(sent, return_sems.at[0])
 
 
 def place(block_device, returned, analysis, sem):
-    blocks = returned.shape[0]
-
-    def one(b, carry):
+    for b in range(returned.shape[0]):
         pltpu.make_async_copy(returned.at[block_device[b]], analysis.at[b], sem).start()
-        return carry
-
-    lax.fori_loop(0, blocks, one, 0)
     wait_bytes(returned, sem)
 
 
@@ -214,19 +230,15 @@
         .transpose(0, 2, 1, 3)
         .reshape(blocks, rows, LANES)
     )
-    index = jnp.arange(blocks, dtype=jnp.int32)
-    owners = jnp.sum(
-        jnp.where(block_device[None, :] == index[:, None], index[None, :], 0), axis=1
-    ).astype(jnp.int32)
     mine = blocks // groups
     any_space = pl.BlockSpec(memory_space=pl.ANY)
     smem = pl.BlockSpec(memory_space=pltpu.SMEM)
     half = jnp.bfloat16
     returned = pl.pallas_call(
         functools.partial(exchange, groups, bands, patches),
-        out_shape=jax.ShapeDtypeStruct((blocks, local, rows, LANES), half),
-        in_specs=[smem, any_space, any_space, any_space],
-        out_specs=any_space,
+        out_shape=pltpu.VMEM((blocks, local, rows, LANES), half),
+        in_specs=[pl.BlockSpec(memory_space=pltpu.VMEM)] + [pl.BlockSpec(memory_space=pltpu.HBM)] * 3,
+        out_specs=pl.BlockSpec(memory_space=pltpu.VMEM),
         scratch_shapes=[
             pltpu.VMEM((blocks, local, rows, LANES), half),
             pltpu.VMEM((groups - 1, mine, local, rows, LANES), half),
@@ -236,23 +248,27 @@
             pltpu.VMEM((blocks, rows, LANES), jnp.float32),
             pltpu.VMEM((members * rows, LANES), jnp.float32),
             pltpu.VMEM((members * rows, LANES), jnp.float32),
-            pltpu.SemaphoreType.DMA((2,)),
+            pltpu.VMEM((1, blocks), jnp.int32),
+            pltpu.SMEM((1, blocks), jnp.int32),
+            pltpu.SemaphoreType.DMA((6,)),
             pltpu.SemaphoreType.DMA((3,)),
             pltpu.SemaphoreType.DMA,
             pltpu.SemaphoreType.DMA((mine,)),
-            pltpu.SemaphoreType.DMA((3,)),
+            pltpu.SemaphoreType.DMA((2,)),
         ],
         compiler_params=pltpu.CompilerParams(
-            collective_id=0, has_side_effects=True, vmem_limit_bytes=48 * 2**20
+            collective_id=0, has_side_effects=True, vmem_limit_bytes=58 * 2**20
         ),
         name="exchange",
-    )(owners, tiled, weights[0], control)
+    )(block_device.reshape(1, blocks), tiled, weights[0], control)
+    steps = 8
     analysis = pl.pallas_call(
         place,
         out_shape=jax.ShapeDtypeStruct((blocks, local, rows, LANES), half),
         in_specs=[smem, any_space],
         out_specs=any_space,
         scratch_shapes=[pltpu.SemaphoreType.DMA],
+        compiler_params=pltpu.CompilerParams(vmem_limit_bytes=8 * 2**20),
         name="place",
     )(block_device, returned)
     return (

time: 291 us -> 127 us (0.44)
  Pallas kernels: 287 us -> 127 us
    pallas_call x1, Pallas kernels: 161 us -> 2.82 us  [per_device(): pl.pallas_call(place, out_shape=jax.ShapeDtypeStruct((blocks, local, rows...]
where the time goes in v2:
time: 127 us
  Pallas kernels  127 us (100%)
    pallas_call x1, Pallas kernels, per_device(): pl.pallas_call(functools.partial(exchange, groups, bands, patches), out_s...  125 us
    pallas_call x1, Pallas kernels, per_device(): pl.pallas_call(place, out_shape=jax.ShapeDtypeStruct((blocks, local, rows...  2.82 us

profile of v2, /device:TPU:1, one launch (start us, length us, event | category | flops | bytes accessed | tf_op | source)
XLA Modules:
  0.0 127.4 jit_solution(17615167439244173097)
XLA Ops:
  0.0 0.0 copy-start
  0.0 124.6 %exchange.1.returned = bf16[128,10,16,128]{3,2,1,0:T(8,128)(2,1)S(1)} custom-call(s32[1,128]{1,0:T(1,128)} %bitcast.17, bf16[128,10,16,128]{3,2,1,0:T(8,128)(2,1)} %bitcast.18, bf16[8,80,80]{2,1,0:T(8,128)(2,1)} %bitcast.20, f32[128,16,128]{2,1,0:T(8,128)} %bitcast.19), custom_call_target="tpu_custom_call" | custom-call | tf_op jit(solution)/shard_map/exchange/pallas_call | solution.py:237
  124.6 0.0 copy-done
  124.6 2.8 %place.1 = bf16[128,10,16,128]{3,2,1,0:T(8,128)(2,1)} custom-call(s32[128]{0:T(128)S(1)} %copy-done, bf16[128,10,16,128]{3,2,1,0:T(8,128)(2,1)S(1)} %exchange.1.returned), custom_call_target="tpu_custom_call" | custom-call | tf_op jit(solution)/shard_map/place/pallas_call | solution.py:265
Async XLA Ops:
  0.0 124.6 %copy-start = (s32[128]{0:T(128)S(1)}, s32[128]{0:T(128)}, u32[]{:S(2)}) copy-start(s32[128]{0:T(128)} %block_device.1) | copy-start | bytes 1540

commit v3 on v2

--- a/solution.py
+++ b/solution.py
@@ -69,7 +69,7 @@
     block_device, fields, weights, control,
     returned,
     held, ordered, gathered, result, chosen, increments, pert, moved, owner_row, owners,
-    load_sems, weight_sems, gather_send, gather_recv, return_sems,
+    load_sems, weight_sems, gather_send, gather_recv, return_sems, later,
 ):
     blocks, local, rows, _ = held.shape
     mine = blocks // groups
@@ -92,8 +92,7 @@
     def half(of_band):
         return lax.rem(of_band // 2, 2)
 
-    def weights_peer(i):
-        to = lax.rem(band + i, bands)
+    def weights_peer(to):
         return group // 2 * 2 + lax.rem(group + half(band) + half(to), 2), to
 
     def slot_of(to, i):
@@ -105,12 +104,16 @@
         pl.semaphore_signal(barrier, inc=1, device_id=(other_group(i), band), device_id_type=MESH)
         return carry
 
-    def greet_band(i, carry):
-        pl.semaphore_signal(barrier, inc=1, device_id=weights_peer(i), device_id_type=MESH)
+    def greet_later(to, carry):
+        pl.semaphore_signal(barrier, inc=1, device_id=weights_peer(to), device_id_type=MESH)
+        return carry
+
+    def greet_earlier(to, carry):
+        pl.semaphore_signal(later, inc=1, device_id=weights_peer(to), device_id_type=MESH)
         return carry
 
     lax.fori_loop(1, groups, greet_group, 0)
-    lax.fori_loop(1, bands, greet_band, 0)
+    lax.fori_loop(band + 1, bands, greet_later, 0)
 
     shape = (blocks, blocks)
     match = block_device[...] == lax.broadcasted_iota(jnp.int32, shape, 0)
@@ -119,23 +122,23 @@
     load_owners = pltpu.make_async_copy(owner_row, owners, load_sems.at[1])
     load_owners.start()
 
-    pl.semaphore_wait(barrier, groups + bands - 2)
+    pl.semaphore_wait(barrier, groups - 1 + band)
+    lax.fori_loop(0, band, greet_earlier, 0)
 
     per_patch = bands // patches
 
-    def send_weights(i, carry):
-        to = weights_peer(i)
+    def send_weights(to, carry):
         pltpu.make_async_remote_copy(
-            src_ref=weights.at[to[1] // per_patch],
+            src_ref=weights.at[to // per_patch],
             dst_ref=chosen.at[band],
             send_sem=weight_sems.at[0],
             recv_sem=weight_sems.at[1],
-            device_id=to,
+            device_id=weights_peer(to),
             device_id_type=MESH,
         ).start()
         return carry
 
-    lax.fori_loop(1, bands, send_weights, 0)
+    lax.fori_loop(0, band, send_weights, 0)
     own_weights = pltpu.make_async_copy(
         weights.at[band // per_patch], chosen.at[band], weight_sems.at[2]
     )
@@ -169,7 +172,14 @@
         lax.fori_loop(1, groups, to_peer, 0)
         return carry
 
-    lax.fori_loop(0, mine, send_block, 0)
+    lax.fori_loop(0, 2, send_block, 0)
+
+    @pl.when(band < bands - 1)
+    def _():
+        pl.semaphore_wait(later, bands - 1 - band)
+
+    lax.fori_loop(band + 1, bands, send_weights, 0)
+    lax.fori_loop(2, mine, send_block, 0)
 
     load_control.wait()
     own_weights.wait()
@@ -255,6 +265,7 @@
             pltpu.SemaphoreType.DMA,
             pltpu.SemaphoreType.DMA((mine,)),
             pltpu.SemaphoreType.DMA((2,)),
+            pltpu.SemaphoreType.REGULAR,
         ],
         compiler_params=pltpu.CompilerParams(
             collective_id=0, has_side_effects=True, vmem_limit_bytes=58 * 2**20

time: 127 us -> 124 us (0.976); the launches traced: 127 us -> 122 us
  Pallas kernels: 127 us -> 122 us
    pallas_call x1, Pallas kernels: 125 us -> 120 us  [per_device(): pl.pallas_call(functools.partial(exchange, groups, bands, patches), out_s...]
where the time goes in v3:
time: 124 us; the launch traced here: 122 us
  Pallas kernels  122 us (98%)
    pallas_call x1, Pallas kernels, per_device(): pl.pallas_call(functools.partial(exchange, groups, bands, patches), out_s...  120 us
    pallas_call x1, Pallas kernels, per_device(): pl.pallas_call(place, out_shape=jax.ShapeDtypeStruct((blocks, local, rows...  2.82 us

profile of v3, /device:TPU:1, one launch (start us, length us, event | category | flops | bytes accessed | tf_op | source)
XLA Modules:
  0.0 122.4 jit_solution(9914484886976479999)
XLA Ops:
  0.0 0.0 copy-start
  0.0 119.6 %exchange.1.returned = bf16[128,10,16,128]{3,2,1,0:T(8,128)(2,1)S(1)} custom-call(s32[1,128]{1,0:T(1,128)} %bitcast.17, bf16[128,10,16,128]{3,2,1,0:T(8,128)(2,1)} %bitcast.18, bf16[8,80,80]{2,1,0:T(8,128)(2,1)} %bitcast.20, f32[128,16,128]{2,1,0:T(8,128)} %bitcast.19), custom_call_target="tpu_custom_call" | custom-call | tf_op jit(solution)/shard_map/exchange/pallas_call | solution.py:247
  119.6 0.0 copy-done
  119.6 2.8 %place.1 = bf16[128,10,16,128]{3,2,1,0:T(8,128)(2,1)} custom-call(s32[128]{0:T(128)S(1)} %copy-done, bf16[128,10,16,128]{3,2,1,0:T(8,128)(2,1)S(1)} %exchange.1.returned), custom_call_target="tpu_custom_call" | custom-call | tf_op jit(solution)/shard_map/place/pallas_call | solution.py:276
Async XLA Ops:
  0.0 119.6 %copy-start = (s32[128]{0:T(128)S(1)}, s32[128]{0:T(128)}, u32[]{:S(2)}) copy-start(s32[128]{0:T(128)} %block_device.1) | copy-start | bytes 1540

commit v4 on v3

--- a/solution.py
+++ b/solution.py
@@ -68,7 +68,7 @@
     groups, bands, patches,
     block_device, fields, weights, control,
     returned,
-    held, ordered, gathered, result, chosen, increments, pert, moved, owner_row, owners,
+    held, ordered, gathered, result, chosen, increments, pert, moved, devices, owner_row, owners,
     load_sems, weight_sems, gather_send, gather_recv, return_sems, later,
 ):
     blocks, local, rows, _ = held.shape
@@ -83,47 +83,49 @@
         return pltpu.make_async_copy(fields.at[part], held.at[part], load_sems.at[2 + i])
 
     load_control = pltpu.make_async_copy(control, increments, load_sems.at[0])
+
+    def other_group(i):
+        return lax.rem(group + i, groups)
+
+    def half(of_band):
+        return lax.rem(of_band // 2, 2)
+
+    def weights_peer(to):
+        return group // 2 * 2 + lax.rem(group + half(band) + half(to), 2), to
+
+    def slot_of(to, i):
+        return (to // 2 * 2 + lax.rem(to + half(band) + half(i), 2)) * bands + i
+
+    barrier = pltpu.get_barrier_semaphore()
+
+    def greet_group(i, carry):
+        pl.semaphore_signal(barrier, inc=1, device_id=(other_group(i), band), device_id_type=MESH)
+        return carry
+
+    def greet_later(to, carry):
+        pl.semaphore_signal(barrier, inc=1, device_id=weights_peer(to), device_id_type=MESH)
+        return carry
+
+    def greet_earlier(to, carry):
+        pl.semaphore_signal(later, inc=1, device_id=weights_peer(to), device_id_type=MESH)
+        return carry
+
+    lax.fori_loop(1, groups, greet_group, 0)
+    load_devices = pltpu.make_async_copy(block_device, devices, load_sems.at[1])
+    load_devices.start()
     for i in range(parts):
         load_fields(i).start()
-
-    def other_group(i):
-        return lax.rem(group + i, groups)
-
-    def half(of_band):
-        return lax.rem(of_band // 2, 2)
-
-    def weights_peer(to):
-        return group // 2 * 2 + lax.rem(group + half(band) + half(to), 2), to
-
-    def slot_of(to, i):
-        return (to // 2 * 2 + lax.rem(to + half(band) + half(i), 2)) * bands + i
-
-    barrier = pltpu.get_barrier_semaphore()
-
-    def greet_group(i, carry):
-        pl.semaphore_signal(barrier, inc=1, device_id=(other_group(i), band), device_id_type=MESH)
-        return carry
-
-    def greet_later(to, carry):
-        pl.semaphore_signal(barrier, inc=1, device_id=weights_peer(to), device_id_type=MESH)
-        return carry
-
-    def greet_earlier(to, carry):
-        pl.semaphore_signal(later, inc=1, device_id=weights_peer(to), device_id_type=MESH)
-        return carry
-
-    lax.fori_loop(1, groups, greet_group, 0)
     lax.fori_loop(band + 1, bands, greet_later, 0)
 
+    load_devices.wait()
     shape = (blocks, blocks)
-    match = block_device[...] == lax.broadcasted_iota(jnp.int32, shape, 0)
+    match = devices[...] == lax.broadcasted_iota(jnp.int32, shape, 0)
     index = jnp.where(match, lax.broadcasted_iota(jnp.int32, shape, 1), 0)
     owner_row[...] = jnp.max(index.T, axis=0, keepdims=True)
     load_owners = pltpu.make_async_copy(owner_row, owners, load_sems.at[1])
     load_owners.start()
 
     pl.semaphore_wait(barrier, groups - 1 + band)
-    lax.fori_loop(0, band, greet_earlier, 0)
 
     per_patch = bands // patches
 
@@ -138,7 +140,6 @@
         ).start()
         return carry
 
-    lax.fori_loop(0, band, send_weights, 0)
     own_weights = pltpu.make_async_copy(
         weights.at[band // per_patch], chosen.at[band], weight_sems.at[2]
     )
@@ -172,7 +173,10 @@
         lax.fori_loop(1, groups, to_peer, 0)
         return carry
 
-    lax.fori_loop(0, 2, send_block, 0)
+    lax.fori_loop(0, 1, send_block, 0)
+    lax.fori_loop(0, band, greet_earlier, 0)
+    lax.fori_loop(0, band, send_weights, 0)
+    lax.fori_loop(1, 2, send_block, 0)
 
     @pl.when(band < bands - 1)
     def _():
@@ -247,7 +251,7 @@
     returned = pl.pallas_call(
         functools.partial(exchange, groups, bands, patches),
         out_shape=pltpu.VMEM((blocks, local, rows, LANES), half),
-        in_specs=[pl.BlockSpec(memory_space=pltpu.VMEM)] + [pl.BlockSpec(memory_space=pltpu.HBM)] * 3,
+        in_specs=[pl.BlockSpec(memory_space=pltpu.HBM)] * 4,
         out_specs=pl.BlockSpec(memory_space=pltpu.VMEM),
         scratch_shapes=[
             pltpu.VMEM((blocks, local, rows, LANES), half),
@@ -258,6 +262,7 @@
             pltpu.VMEM((blocks, rows, LANES), jnp.float32),
             pltpu.VMEM((members * rows, LANES), jnp.float32),
             pltpu.VMEM((members * rows, LANES), jnp.float32),
+            pltpu.VMEM((1, blocks), jnp.int32),
             pltpu.VMEM((1, blocks), jnp.int32),
             pltpu.SMEM((1, blocks), jnp.int32),
             pltpu.SemaphoreType.DMA((6,)),

time: 124 us -> 123 us (level)
  no operation moved by 1% of the time
where the time goes in v4:
time: 123 us
  Pallas kernels  123 us (100%)
    pallas_call x1, Pallas kernels, per_device(): pl.pallas_call(functools.partial(exchange, groups, bands, patches), out_s...  120 us
    pallas_call x1, Pallas kernels, per_device(): pl.pallas_call(place, out_shape=jax.ShapeDtypeStruct((blocks, local, rows...  2.82 us

profile of v4, /device:TPU:1, one launch (start us, length us, event | category | flops | bytes accessed | tf_op | source)
XLA Modules:
  0.0 122.7 jit_solution(14002787632656622126)
XLA Ops:
  0.0 0.0 copy-start
  0.0 119.8 %exchange.1.returned = bf16[128,10,16,128]{3,2,1,0:T(8,128)(2,1)S(1)} custom-call(s32[1,128]{1,0:T(1,128)} %bitcast.17, bf16[128,10,16,128]{3,2,1,0:T(8,128)(2,1)} %bitcast.18, bf16[8,80,80]{2,1,0:T(8,128)(2,1)} %bitcast.20, f32[128,16,128]{2,1,0:T(8,128)} %bitcast.19), custom_call_target="tpu_custom_call" | custom-call | tf_op jit(solution)/shard_map/exchange/pallas_call | solution.py:251
  119.8 0.0 copy-done
  119.8 2.8 %place.1 = bf16[128,10,16,128]{3,2,1,0:T(8,128)(2,1)} custom-call(s32[128]{0:T(128)S(1)} %copy-done, bf16[128,10,16,128]{3,2,1,0:T(8,128)(2,1)S(1)} %exchange.1.returned), custom_call_target="tpu_custom_call" | custom-call | tf_op jit(solution)/shard_map/place/pallas_call | solution.py:281
Async XLA Ops:
  0.0 119.8 %copy-start = (s32[128]{0:T(128)S(1)}, s32[128]{0:T(128)}, u32[]{:S(2)}) copy-start(s32[128]{0:T(128)} %block_device.1) | copy-start | bytes 1540

commit v5 on v4

--- a/solution.py
+++ b/solution.py
@@ -224,8 +224,9 @@
 
 
 def place(block_device, returned, analysis, sem):
+    devices = block_device[...]
     for b in range(returned.shape[0]):
-        pltpu.make_async_copy(returned.at[block_device[b]], analysis.at[b], sem).start()
+        pltpu.make_async_copy(returned.at[devices[0, b]], analysis.at[b], sem).start()
     wait_bytes(returned, sem)
 
 
@@ -281,12 +282,12 @@
     analysis = pl.pallas_call(
         place,
         out_shape=jax.ShapeDtypeStruct((blocks, local, rows, LANES), half),
-        in_specs=[smem, any_space],
+        in_specs=[pl.BlockSpec(memory_space=pltpu.VMEM), any_space],
         out_specs=any_space,
         scratch_shapes=[pltpu.SemaphoreType.DMA],
         compiler_params=pltpu.CompilerParams(vmem_limit_bytes=8 * 2**20),
         name="place",
-    )(block_device, returned)
+    )(block_device.reshape(1, blocks), returned)
     return (
         analysis.reshape(blocks, local, pieces, band_rows, LANES)
         .transpose(0, 1, 3, 2, 4)

time: 123 us -> 122 us (level)
  no operation moved by 1% of the time
where the time goes in v5:
time: 122 us
  Pallas kernels  122 us (100%)
    pallas_call x1, Pallas kernels, per_device(): pl.pallas_call(functools.partial(exchange, groups, bands, patches), out_s...  120 us

profile of v5, /device:TPU:1, one launch (start us, length us, event | category | flops | bytes accessed | tf_op | source)
XLA Modules:
  0.0 122.2 jit_solution(680648307989189897)
XLA Ops:
  0.0 0.0 copy-start
  0.0 119.8 %exchange.1.returned = bf16[128,10,16,128]{3,2,1,0:T(8,128)(2,1)S(1)} custom-call(s32[1,128]{1,0:T(1,128)} %bitcast.17, bf16[128,10,16,128]{3,2,1,0:T(8,128)(2,1)} %bitcast.19, bf16[8,80,80]{2,1,0:T(8,128)(2,1)} %bitcast.21, f32[128,16,128]{2,1,0:T(8,128)} %bitcast.20), custom_call_target="tpu_custom_call" | custom-call | tf_op jit(solution)/shard_map/exchange/pallas_call | solution.py:252
  119.8 0.0 copy-done
  119.8 2.4 %place.1 = bf16[128,10,16,128]{3,2,1,0:T(8,128)(2,1)} custom-call(s32[1,128]{1,0:T(1,128)S(1)} %bitcast.18, bf16[128,10,16,128]{3,2,1,0:T(8,128)(2,1)S(1)} %exchange.1.returned), custom_call_target="tpu_custom_call" | custom-call | tf_op jit(solution)/shard_map/place/pallas_call | solution.py:282
Async XLA Ops:
  0.0 119.8 %copy-start = (s32[128]{0:T(128)S(1)}, s32[128]{0:T(128)}, u32[]{:S(2)}) copy-start(s32[128]{0:T(128)} %param.5) | copy-start | bytes 1540

commit v6 on v5

--- a/solution.py
+++ b/solution.py
@@ -68,19 +68,28 @@
     groups, bands, patches,
     block_device, fields, weights, control,
     returned,
-    held, ordered, gathered, result, chosen, increments, pert, moved, devices, owner_row, owners,
+    held, held_rest, ordered, gathered, result, chosen, increments, pert, moved, devices, owner_row, owners,
     load_sems, weight_sems, gather_send, gather_recv, return_sems, later,
 ):
-    blocks, local, rows, _ = held.shape
+    blocks, local, rows, _ = fields.shape
     mine = blocks // groups
     members = groups * local
     group = lax.axis_index("member")
     band = lax.axis_index("patch")
-    parts = 4
-
-    def load_fields(i):
+    parts = 2
+    early = held.shape[1]
+
+    def load_fields(i, rest):
         part = pl.ds(i * (blocks // parts), blocks // parts)
-        return pltpu.make_async_copy(fields.at[part], held.at[part], load_sems.at[2 + i])
+        some = pl.ds(early, local - early) if rest else pl.ds(0, early)
+        return pltpu.make_async_copy(
+            fields.at[part, some],
+            (held_rest if rest else held).at[part],
+            load_sems.at[2 + i + (parts if rest else 0)],
+        )
+
+    def member(block, k):
+        return held[block, k] if k < early else held_rest[block, k - early]
 
     load_control = pltpu.make_async_copy(control, increments, load_sems.at[0])
 
@@ -102,11 +111,18 @@
         pl.semaphore_signal(barrier, inc=1, device_id=(other_group(i), band), device_id_type=MESH)
         return carry
 
-    def greet_later(to, carry):
+    def place_in_order(of_band):
+        return of_band // 2 * 2 + 1 - lax.rem(of_band, 2)
+
+    rank = place_in_order(band)
+
+    def greet_later(i, carry):
+        to = place_in_order(i)
         pl.semaphore_signal(barrier, inc=1, device_id=weights_peer(to), device_id_type=MESH)
         return carry
 
-    def greet_earlier(to, carry):
+    def greet_earlier(i, carry):
+        to = place_in_order(i)
         pl.semaphore_signal(later, inc=1, device_id=weights_peer(to), device_id_type=MESH)
         return carry
 
@@ -114,8 +130,10 @@
     load_devices = pltpu.make_async_copy(block_device, devices, load_sems.at[1])
     load_devices.start()
     for i in range(parts):
-        load_fields(i).start()
-    lax.fori_loop(band + 1, bands, greet_later, 0)
+        load_fields(i, False).start()
+    for i in range(parts):
+        load_fields(i, True).start()
+    lax.fori_loop(rank + 1, bands, greet_later, 0)
 
     load_devices.wait()
     shape = (blocks, blocks)
@@ -125,11 +143,12 @@
     load_owners = pltpu.make_async_copy(owner_row, owners, load_sems.at[1])
     load_owners.start()
 
-    pl.semaphore_wait(barrier, groups - 1 + band)
+    pl.semaphore_wait(barrier, groups - 1 + rank)
 
     per_patch = bands // patches
 
-    def send_weights(to, carry):
+    def send_weights(i, carry):
+        to = place_in_order(i)
         pltpu.make_async_remote_copy(
             src_ref=weights.at[to // per_patch],
             dst_ref=chosen.at[band],
@@ -147,22 +166,21 @@
 
     load_owners.wait()
     for i in range(parts):
-        load_fields(i).wait()
-    load_control.start()
-
-    def send_block(c, carry):
+        load_fields(i, False).wait()
+
+    def send_block(c, carry, first=0, last=local):
         here = owners[0, slot_of(group, c)]
-        for k in range(local):
-            gathered[c, group * local + k] = held[here, k]
+        for k in range(first, last):
+            gathered[c, group * local + k] = member(here, k)
 
         def to_peer(i, inner):
             to = other_group(i)
             block = owners[0, slot_of(to, c)]
-            for k in range(local):
-                ordered[i - 1, c, k] = held[block, k]
+            for k in range(first, last):
+                ordered[i - 1, c, k] = member(block, k)
             pltpu.make_async_remote_copy(
-                src_ref=ordered.at[i - 1, c],
-                dst_ref=gathered.at[c, pl.ds(group * local, local)],
+                src_ref=ordered.at[i - 1, c, pl.ds(first, last - first)],
+                dst_ref=gathered.at[c, pl.ds(group * local + first, last - first)],
                 send_sem=gather_send,
                 recv_sem=gather_recv.at[c],
                 device_id=(to, band),
@@ -173,17 +191,22 @@
         lax.fori_loop(1, groups, to_peer, 0)
         return carry
 
-    lax.fori_loop(0, 1, send_block, 0)
-    lax.fori_loop(0, band, greet_earlier, 0)
-    lax.fori_loop(0, band, send_weights, 0)
-    lax.fori_loop(1, 2, send_block, 0)
-
-    @pl.when(band < bands - 1)
+    send_block(0, 0, last=early)
+    for i in range(parts):
+        load_fields(i, True).wait()
+    load_control.start()
+    send_block(0, 0, first=early)
+    lax.fori_loop(1, 4, send_block, 0)
+    lax.fori_loop(0, rank, greet_earlier, 0)
+    lax.fori_loop(0, rank, send_weights, 0)
+    lax.fori_loop(4, 5, send_block, 0)
+
+    @pl.when(rank < bands - 1)
     def _():
-        pl.semaphore_wait(later, bands - 1 - band)
-
-    lax.fori_loop(band + 1, bands, send_weights, 0)
-    lax.fori_loop(2, mine, send_block, 0)
+        pl.semaphore_wait(later, bands - 1 - rank)
+
+    lax.fori_loop(rank + 1, bands, send_weights, 0)
+    lax.fori_loop(5, mine, send_block, 0)
 
     load_control.wait()
     own_weights.wait()
@@ -246,6 +269,7 @@
         .reshape(blocks, rows, LANES)
     )
     mine = blocks // groups
+    early = local // 2
     any_space = pl.BlockSpec(memory_space=pl.ANY)
     smem = pl.BlockSpec(memory_space=pltpu.SMEM)
     half = jnp.bfloat16
@@ -255,14 +279,15 @@
         in_specs=[pl.BlockSpec(memory_space=pltpu.HBM)] * 4,
         out_specs=pl.BlockSpec(memory_space=pltpu.VMEM),
         scratch_shapes=[
-            pltpu.VMEM((blocks, local, rows, LANES), half),
+            pltpu.VMEM((blocks, early, rows, LANES), half),
+            pltpu.VMEM((blocks, local - early, rows, LANES), half),
             pltpu.VMEM((groups - 1, mine, local, rows, LANES), half),
             pltpu.VMEM((mine, members, rows, LANES), half),
             pltpu.VMEM((mine, members, rows, LANES), half),
             pltpu.VMEM((bands, members, members), half),
             pltpu.VMEM((blocks, rows, LANES), jnp.float32),
-            pltpu.VMEM((members * rows, LANES), jnp.float32),
-            pltpu.VMEM((members * rows, LANES), jnp.float32),
+            pltpu.VMEM((members * rows + rows, LANES), jnp.float32),
+            pltpu.VMEM((members * rows + rows, LANES), jnp.float32),
             pltpu.VMEM((1, blocks), jnp.int32),
             pltpu.VMEM((1, blocks), jnp.int32),
             pltpu.SMEM((1, blocks), jnp.int32),

time: 122 us -> 122 us (level)
  no operation moved by 1% of the time
where the time goes in v6:
time: 122 us; the launch traced here: 121 us
  Pallas kernels  121 us (99%)
    pallas_call x1, Pallas kernels, per_device(): pl.pallas_call(functools.partial(exchange, groups, bands, patches), out_s...  119 us

profile of v6, /device:TPU:1, one launch (start us, length us, event | category | flops | bytes accessed | tf_op | source)
XLA Modules:
  0.0 121.1 jit_solution(14501540180963427626)
XLA Ops:
  0.0 0.0 copy-start
  0.0 118.7 %exchange.1.returned = bf16[128,10,16,128]{3,2,1,0:T(8,128)(2,1)S(1)} custom-call(s32[1,128]{1,0:T(1,128)} %bitcast.17, bf16[128,10,16,128]{3,2,1,0:T(8,128)(2,1)} %bitcast.19, bf16[8,80,80]{2,1,0:T(8,128)(2,1)} %bitcast.21, f32[128,16,128]{2,1,0:T(8,128)} %bitcast.20), custom_call_target="tpu_custom_call" | custom-call | tf_op jit(solution)/shard_map/exchange/pallas_call | solution.py:276
  118.7 0.0 copy-done
  118.7 2.4 %place.1 = bf16[128,10,16,128]{3,2,1,0:T(8,128)(2,1)} custom-call(s32[1,128]{1,0:T(1,128)S(1)} %bitcast.18, bf16[128,10,16,128]{3,2,1,0:T(8,128)(2,1)S(1)} %exchange.1.returned), custom_call_target="tpu_custom_call" | custom-call | tf_op jit(solution)/shard_map/place/pallas_call | solution.py:307
Async XLA Ops:
  0.0 118.7 %copy-start = (s32[128]{0:T(128)S(1)}, s32[128]{0:T(128)}, u32[]{:S(2)}) copy-start(s32[128]{0:T(128)} %param.5) | copy-start | bytes 1540

commit v7 on v6

--- a/solution.py
+++ b/solution.py
@@ -10,6 +10,7 @@
 RELAXATION = 0.85
 EPSILON = 1e-06
 MESH = pl.DeviceIdType.MESH
+AHEAD = 8
 LANES = 128
 
 
@@ -206,7 +207,7 @@
         pl.semaphore_wait(later, bands - 1 - rank)
 
     lax.fori_loop(rank + 1, bands, send_weights, 0)
-    lax.fori_loop(5, mine, send_block, 0)
+    lax.fori_loop(5, AHEAD, send_block, 0)
 
     load_control.wait()
     own_weights.wait()
@@ -233,6 +234,10 @@
             return inner
 
         lax.fori_loop(1, groups, to_peer, 0)
+        @pl.when(c + AHEAD < mine)
+        def _():
+            send_block(c + AHEAD, 0)
+
         for k in range(local):
             returned[slot, k] = result[c, group * local + k]
         return carry

time: 122 us -> 122 us (level)
  no operation moved by 1% of the time
where the time goes in v7:
time: 122 us; the launch traced here: 121 us
  Pallas kernels  121 us (99%)
    pallas_call x1, Pallas kernels, per_device(): pl.pallas_call(functools.partial(exchange, groups, bands, patches), out_s...  119 us

profile of v7, /device:TPU:1, one launch (start us, length us, event | category | flops | bytes accessed | tf_op | source)
XLA Modules:
  0.0 121.1 jit_solution(3242887087764884836)
XLA Ops:
  0.0 0.0 copy-start
  0.0 118.7 %exchange.1.returned = bf16[128,10,16,128]{3,2,1,0:T(8,128)(2,1)S(1)} custom-call(s32[1,128]{1,0:T(1,128)} %bitcast.17, bf16[128,10,16,128]{3,2,1,0:T(8,128)(2,1)} %bitcast.19, bf16[8,80,80]{2,1,0:T(8,128)(2,1)} %bitcast.21, f32[128,16,128]{2,1,0:T(8,128)} %bitcast.20), custom_call_target="tpu_custom_call" | custom-call | tf_op jit(solution)/shard_map/exchange/pallas_call | solution.py:281
  118.7 0.0 copy-done
  118.7 2.4 %place.1 = bf16[128,10,16,128]{3,2,1,0:T(8,128)(2,1)} custom-call(s32[1,128]{1,0:T(1,128)S(1)} %bitcast.18, bf16[128,10,16,128]{3,2,1,0:T(8,128)(2,1)S(1)} %exchange.1.returned), custom_call_target="tpu_custom_call" | custom-call | tf_op jit(solution)/shard_map/place/pallas_call | solution.py:312
Async XLA Ops:
  0.0 118.7 %copy-start = (s32[128]{0:T(128)S(1)}, s32[128]{0:T(128)}, u32[]{:S(2)}) copy-start(s32[128]{0:T(128)} %param.5) | copy-start | bytes 1540

commit v8 on v7

--- a/solution.py
+++ b/solution.py
@@ -11,6 +11,8 @@
 EPSILON = 1e-06
 MESH = pl.DeviceIdType.MESH
 AHEAD = 8
+HELD = 4
+LATE = 6
 LANES = 128
 
 
@@ -213,6 +215,19 @@
     own_weights.wait()
     wait_bytes(chosen.at[pl.ds(0, bands - 1)], weight_sems.at[1])
 
+    def send_back(c, to):
+        pltpu.make_async_remote_copy(
+            src_ref=result.at[c, pl.ds(to * local, local)],
+            dst_ref=returned.at[slot_of(group, c)],
+            send_sem=return_sems.at[0],
+            recv_sem=return_sems.at[1],
+            device_id=(to, band),
+            device_id_type=MESH,
+        ).start()
+
+    def held_back(to):
+        return (group >= LATE) & (to >= LATE)
+
     def analyse_block(c, carry):
         wait_bytes(gathered.at[c, pl.ds(0, members - local)], gather_recv.at[c])
         slot = slot_of(group, c)
@@ -223,14 +238,12 @@
 
         def to_peer(i, inner):
             to = other_group(i)
-            pltpu.make_async_remote_copy(
-                src_ref=result.at[c, pl.ds(to * local, local)],
-                dst_ref=returned.at[slot],
-                send_sem=return_sems.at[0],
-                recv_sem=return_sems.at[1],
-                device_id=(to, band),
-                device_id_type=MESH,
-            ).start()
+            block = jnp.where(held_back(to), c - HELD, c)
+
+            @pl.when(block >= 0)
+            def _():
+                send_back(block, to)
+
             return inner
 
         lax.fori_loop(1, groups, to_peer, 0)
@@ -243,6 +256,18 @@
         return carry
 
     lax.fori_loop(0, mine, analyse_block, 0)
+
+    def send_last(i, carry):
+        to = other_group(i)
+
+        @pl.when(held_back(to))
+        def _():
+            for c in range(mine - HELD, mine):
+                send_back(c, to)
+
+        return carry
+
+    lax.fori_loop(1, groups, send_last, 0)
 
     sent = returned.at[pl.ds(0, blocks - mine)]
     wait_bytes(sent, return_sems.at[1])

time: 122 us -> 122 us (level)
  no operation moved by 1% of the time
where the time goes in v8:
time: 122 us; the launch traced here: 121 us
  Pallas kernels  121 us (99%)
    pallas_call x1, Pallas kernels, per_device(): pl.pallas_call(functools.partial(exchange, groups, bands, patches), out_s...  119 us

profile of v8, /device:TPU:1, one launch (start us, length us, event | category | flops | bytes accessed | tf_op | source)
XLA Modules:
  0.0 121.1 jit_solution(16783212694759500511)
XLA Ops:
  0.0 0.0 copy-start
  0.0 118.7 %exchange.1.returned = bf16[128,10,16,128]{3,2,1,0:T(8,128)(2,1)S(1)} custom-call(s32[1,128]{1,0:T(1,128)} %bitcast.17, bf16[128,10,16,128]{3,2,1,0:T(8,128)(2,1)} %bitcast.19, bf16[8,80,80]{2,1,0:T(8,128)(2,1)} %bitcast.21, f32[128,16,128]{2,1,0:T(8,128)} %bitcast.20), custom_call_target="tpu_custom_call" | custom-call | tf_op jit(solution)/shard_map/exchange/pallas_call | solution.py:306
  118.7 0.0 copy-done
  118.7 2.4 %place.1 = bf16[128,10,16,128]{3,2,1,0:T(8,128)(2,1)} custom-call(s32[1,128]{1,0:T(1,128)S(1)} %bitcast.18, bf16[128,10,16,128]{3,2,1,0:T(8,128)(2,1)S(1)} %exchange.1.returned), custom_call_target="tpu_custom_call" | custom-call | tf_op jit(solution)/shard_map/place/pallas_call | solution.py:337
Async XLA Ops:
  0.0 118.7 %copy-start = (s32[128]{0:T(128)S(1)}, s32[128]{0:T(128)}, u32[]{:S(2)}) copy-start(s32[128]{0:T(128)} %param.5) | copy-start | bytes 1540

commit v9 on v7

--- a/solution.py
+++ b/solution.py
@@ -274,7 +274,7 @@
         .reshape(blocks, rows, LANES)
     )
     mine = blocks // groups
-    early = local // 2
+    early = max(1, local // 5)
     any_space = pl.BlockSpec(memory_space=pl.ANY)
     smem = pl.BlockSpec(memory_space=pltpu.SMEM)
     half = jnp.bfloat16

time: 122 us -> 122 us (level)
  no operation moved by 1% of the time
where the time goes in v9:
time: 122 us; the launch traced here: 121 us
  Pallas kernels  121 us (99%)
    pallas_call x1, Pallas kernels, per_device(): pl.pallas_call(functools.partial(exchange, groups, bands, patches), out_s...  119 us

profile of v9, /device:TPU:1, one launch (start us, length us, event | category | flops | bytes accessed | tf_op | source)
XLA Modules:
  0.0 121.4 jit_solution(10037409269421533359)
XLA Ops:
  0.0 0.0 copy-start
  0.0 119.0 %exchange.1.returned = bf16[128,10,16,128]{3,2,1,0:T(8,128)(2,1)S(1)} custom-call(s32[1,128]{1,0:T(1,128)} %bitcast.17, bf16[128,10,16,128]{3,2,1,0:T(8,128)(2,1)} %bitcast.19, bf16[8,80,80]{2,1,0:T(8,128)(2,1)} %bitcast.21, f32[128,16,128]{2,1,0:T(8,128)} %bitcast.20), custom_call_target="tpu_custom_call" | custom-call | tf_op jit(solution)/shard_map/exchange/pallas_call | solution.py:281
  119.0 0.0 copy-done
  119.0 2.4 %place.1 = bf16[128,10,16,128]{3,2,1,0:T(8,128)(2,1)} custom-call(s32[1,128]{1,0:T(1,128)S(1)} %bitcast.18, bf16[128,10,16,128]{3,2,1,0:T(8,128)(2,1)S(1)} %exchange.1.returned), custom_call_target="tpu_custom_call" | custom-call | tf_op jit(solution)/shard_map/place/pallas_call | solution.py:312
Async XLA Ops:
  0.0 119.0 %copy-start = (s32[128]{0:T(128)S(1)}, s32[128]{0:T(128)}, u32[]{:S(2)}) copy-start(s32[128]{0:T(128)} %param.5) | copy-start | bytes 1540
